TPU v7x, 32 devices: a whole 2x2x4 slice. The times are simulated.
32 devices in a mesh: prow: 4 (over y, x), pcol: 8 (over z, core).
Axes of the slice: x: 2, y: 2, z: 4, core: 2. Of those that a mesh axis runs over, the one named last changes fastest.
Arguments:
- window: float32 [16384, 16384], P('prow', 'pcol'), may hold values from -6 to 6
- panel: float32 [16384, 256], P(('prow', 'pcol')), may hold values from -0.046875 to 0.046875
- factor: float32 [256, 256], replicated, may hold values from -1 to 1
- col_check: float32 [16384], P('pcol'), may hold values from -6 to 6
- row_check: float32 [16384], P('prow'), may hold values from -6 to 6
Outputs:
- new_window: float32 [16384, 16384], P('prow', 'pcol')
- new_col: float32 [16384], P('pcol')
- new_row: float32 [16384], P('prow')
All inputs are finite; a program needn't handle non-finite values.
Results may differ from a plain program's by a relative error of at most 0.00005.
Values sent between devices are 32-bit elements; how exact they have to be, the bound alone decides.
A program may use at most 128 MiB of HBM per device.

v0:
```python
import math

import jax
import jax.numpy as jnp
from jax import lax
from jax.sharding import PartitionSpec as P

N = 16384


def spread(block, axis, holder):
    block = jnp.where(lax.axis_index(axis) == holder, block, jnp.zeros_like(block))
    return lax.psum(block, axis)


def unit_lower(values, row_start):
    rows = row_start + jnp.arange(values.shape[0], dtype=jnp.int32)[:, None]
    cols = jnp.arange(values.shape[1], dtype=jnp.int32)[None, :]
    ones = jnp.where(rows == cols, jnp.ones_like(values), jnp.zeros_like(values))
    return jnp.where(rows > cols, values, ones)


def matmul(left, right):
    return jnp.dot(left, right, precision=lax.Precision.HIGHEST)


def inner_rows(left, right):
    return lax.dot_general(left, right, (((0,), (0,)), ((), ())), precision=lax.Precision.HIGHEST)


def outer_cols(left, right):
    return lax.dot_general(left, right, (((1,), (1,)), ((), ())), precision=lax.Precision.HIGHEST)


def on_device(window, panel, factor, col_check, row_check):
    n_rows = lax.axis_size("prow")
    n_cols = lax.axis_size("pcol")
    prow_idx = lax.axis_index("prow")
    pcol_idx = lax.axis_index("pcol")
    rows_blk = window.shape[0]
    cols_blk = window.shape[1]
    ratio = n_cols // n_rows
    upper = jnp.triu(factor)
    gathered = lax.all_gather(panel, "pcol", axis=0, tiled=True)
    v_rows = unit_lower(gathered, prow_idx * rows_blk)
    half_part = lax.dynamic_slice_in_dim(gathered, pcol_idx % ratio * cols_blk, cols_blk, 0)
    raw_cols = spread(half_part, "prow", pcol_idx // ratio)
    v_cols = unit_lower(raw_cols, pcol_idx * cols_blk)
    col_proj, col_sums = lax.psum((matmul(col_check, v_cols), jnp.sum(v_cols, axis=0)), "pcol")
    row_part = matmul(row_check, v_rows)
    x_rows = lax.psum(matmul(window, v_cols), "pcol")
    w_trans, row_proj = lax.psum((inner_rows(window, v_rows), row_part), "prow")
    y_rows = matmul(x_rows, upper)
    coupled = lax.psum(inner_rows(v_rows, y_rows), "prow")
    m_trans = matmul(w_trans - outer_cols(v_cols, coupled), upper)
    left = jnp.concatenate([y_rows, v_rows], axis=1)
    right = jnp.concatenate([v_cols, m_trans], axis=1)
    new_window = window - outer_cols(left, right)
    scaled = col_sums / math.sqrt(N)
    new_col = col_check - matmul(v_cols, matmul(col_proj, upper)) - matmul(m_trans, scaled)
    inner = row_proj - matmul(coupled, scaled)
    new_row = row_check - matmul(y_rows, scaled) - matmul(v_rows, matmul(inner, upper))
    return (new_window, new_col, new_row)


def solution(mesh):
    placed = (P("prow", "pcol"), P(("prow", "pcol"), None), P(), P("pcol"), P("prow"))
    return jax.shard_map(
        on_device,
        mesh=mesh,
        in_specs=placed,
        out_specs=(P("prow", "pcol"), P("pcol"), P("prow")),
        check_vma=False,
    )
```

profile of v0, /device:TPU:0, one launch (start us, length us, event | category | flops | bytes accessed | tf_op | source)
XLA Modules:
  0.0 429.2 jit_solution(33930678383725721)
XLA Ops:
  7.2 0.0 all-gather.2.cloned.1.call-start
  7.2 2.0 copy.8
  9.2 0.0 all-gather.2.cloned.1.call-update
  9.3 0.0 all-reduce.6.cloned.1.call-start
  9.3 50.7 %all-gather.2.cloned.1.call-done = f32[4096,256]{0,1:T(8,128)} async-done(((f32[512,256]{0,1:T(8,128)}), f32[4096,256]{0,1:T(8,128)}) %all-gather.2.cloned.1.call-update) | async-done | bytes 4194320 | tf_op jit(solution)/shard_map/all_gather | solution.py:44
  60.1 3.1 dynamic-slice_select_fusion
  63.2 0.0 all-reduce.6.cloned.1.call-update
  63.2 0.0 all-reduce.8.cloned.1.call-start
  63.3 68.8 %all-reduce.6.cloned.1.call-done = f32[2048,256]{0,1:T(8,128)} async-done(((f32[2048,256]{0,1:T(8,128)}), f32[2048,256]{0,1:T(8,128)}) %all-reduce.6.cloned.1.call-update) | async-done | bytes 2097168 | tf_op jit(solution)/shard_map/psum | solution.py:13
  132.1 2.0 fusion.26
  134.2 33.3 %convolution_bitcast_fusion = f32[4096,256]{0,1:T(8,128)} fusion(f32[2048,256]{0,1:T(8,128)S(1)} %get-tuple-element.8, f32[4096,2048]{1,0:T(8,128)} %param.5), kind=kOutput, calls=%fused_computation.4 | convolution fusion | flops 25769803776 | bytes 39845888 | tf_op jit(solution)/shard_map/dot_general | solution.py:24
  167.5 0.0 all-reduce.8.cloned.1.call-update
  167.5 0.2 all-reduce.10.cloned.1.call-start
  167.7 2.7 select_select_fusion
  170.4 0.0 copy-start
  170.5 2.0 copy-done
  172.5 0.0 copy-start.5
  172.5 33.8 %convolution_bitcast_fusion.1 = f32[2048,256]{0,1:T(8,128)} fusion(f32[4096,256]{0,1:T(8,128)S(1)} %select_select_fusion, f32[4096,2048]{1,0:T(8,128)} %param.5), kind=kOutput, calls=%fused_computation.12 | convolution fusion | flops 25769803776 | bytes 39845888 | tf_op jit(solution)/shard_map/dot_general | solution.py:28
  206.3 57.9 %all-reduce.8.cloned.1.call-done = f32[4096,256]{0,1:T(8,128)} async-done(((f32[4096,256]{0,1:T(8,128)}), f32[4096,256]{0,1:T(8,128)}) %all-reduce.8.cloned.1.call-update) | async-done | bytes 4194320 | tf_op jit(solution)/shard_map/psum | solution.py:51
  264.2 0.0 copy-done.5
  264.2 0.0 copy-start.1
  264.2 6.0 %fusion.11 = f32[4096,256]{0,1:T(8,128)S(1)} fusion(f32[4096,256]{0,1:T(8,128)} %all-reduce.8.cloned.1.call-done, f32[256,256]{1,0:T(8,128)S(1)} %copy-done.5, s32[256]{0:T(256)S(1)} %iota_add_fusion.2), kind=kOutput, calls=%fused_computation.22 | convolution fusion | flops 3221356544 | bytes 8651776 | tf_op jit(solution)/shard_map/dot_general | solution.py:24
  270.1 0.0 copy-start.3
  270.2 1.9 copy-done.3
  272.1 0.0 copy-done.1
  272.1 0.0 copy-start.6
  272.1 4.3 fusion.27
  276.4 0.0 copy-start.7
  276.4 0.0 all-reduce.10.cloned.1.call-update
  276.4 0.0 copy-done.6
  276.4 5.5 %fusion.32 = f32[1,256]{1,0:T(1,128)S(1)} fusion(f32[4096,256]{0,1:T(8,128)} %copy-done, f32[4096,1]{0,1:T(1,128)S(1)} %bitcast.50), kind=kOutput, calls=%fused_computation.48 | convolution fusion | flops 12582912 | bytes 4211712 | tf_op jit(solution)/shard_map/dot_general | solution.py:24
  281.9 10.3 %psum.55 = f32[256]{0:T(256)S(1)} all-reduce(f32[256]{0:T(256)S(1)} %bitcast.62), channel_id=1, replica_groups=mesh['prow'=4,'pcol'=8] {'prow'}, use_global_device_ids=true, to_apply=%region_7.8 | all-reduce | flops 256 | bytes 2048 | tf_op jit(solution)/shard_map/psum | solution.py:52
  292.2 0.0 copy-done.7
  292.2 1.7 fusion.28
  294.0 13.6 %all-reduce = (f32[256]{0:T(256)S(1)}, f32[256]{0:T(256)S(1)}) all-reduce(f32[256]{0:T(256)S(1)} %get-tuple-element.7, f32[256]{0:T(256)S(1)} %bitcast.61), channel_id=1, replica_groups=mesh['prow'=4,'pcol'=8] {'pcol'}, use_global_device_ids=true, to_apply=%region_6.7 | all-reduce | flops 512 | bytes 4096 | tf_op jit(solution)/shard_map/psum | solution.py:49
  307.6 0.3 convolution_bitcast_fusion.3
  307.8 1.2 fusion.29
  309.1 4.5 %fusion.31 = f32[1,4096]{1,0:T(1,128)S(1)} fusion(f32[4096,256]{0,1:T(8,128)} %copy-done.3, f32[256,1]{0,1:T(1,128)S(1)} %bitcast.56), kind=kOutput, calls=%fused_computation.47 | convolution fusion | flops 12582912 | bytes 4211712 | tf_op jit(solution)/shard_map/dot_general | solution.py:24
  313.6 37.5 %all-reduce.10.cloned.1.call-done = (f32[2048,256]{0,1:T(8,128)}, f32[256,256]{1,0:T(8,128)}) async-done(((f32[2048,256]{0,1:T(8,128)}, f32[256,256]{1,0:T(8,128)}), (f32[2048,256]{0,1:T(8,128)}, f32[256,256]{1,0:T(8,128)})) %all-reduce.10.cloned.1.call-update) | async-done | bytes 2359312 | tf_op jit(solution)/shard_map/psum | solution.py:52
  351.0 1.2 fusion.33
  352.2 0.0 copy-start.2
  352.2 0.1 copy-start.4
  352.3 3.8 convolution_subtract_fusion.1
  356.1 2.1 fusion.9
  358.3 0.0 copy-done.2
  358.3 0.0 copy-done.4
  358.3 59.0 %convolution_subtract_fusion = f32[4096,2048]{1,0:T(8,128)} fusion(f32[4096,2048]{1,0:T(8,128)} %param.5, f32[4096,256]{0,1:T(8,128)S(1)} %copy-done.2, f32[4096,256]{0,1:T(8,128)S(1)} %copy-done.4, f32[2048,256]{0,1:T(8,128)S(1)} %fusion.9, f32[2048,256]{0,1:T(8,128)S(1)} %get-tuple-element.8), kind=kOutput, calls=%fused_computation | convolution fusion | flops 51551141888 | bytes 79691776 | tf_op jit(solution)/shard_map/dot_general | solution.py:32
  417.3 1.2 fusion.30
  418.5 0.3 convolution_bitcast_fusion.2
  418.7 2.3 fusion.34
  421.0 0.6 subtract_subtract_fusion
  421.7 0.6 subtract_subtract_fusion.1
  (5 shorter events, 0.0 us)
Async XLA Ops:
  7.2 52.9 %all-gather.2.cloned.1.call-start = ((), (), s32[]{:S(2)}) async-start(), calls=%async_computation | async-start | bytes 4718592 | tf_op jit(solution)/shard_map/all_gather | solution.py:44
  9.3 122.9 %all-reduce.6.cloned.1.call-start = ((), (), s32[]{:S(2)}) async-start(), calls=%async_computation.1 | async-start | bytes 4194304 | tf_op jit(solution)/shard_map/psum | solution.py:13
  63.2 200.9 %all-reduce.8.cloned.1.call-start = ((), (), s32[]{:S(2)}) async-start(), calls=%async_computation.2 | async-start | bytes 8388608 | tf_op jit(solution)/shard_map/psum | solution.py:51
  167.5 183.5 %all-reduce.10.cloned.1.call-start = ((), (), s32[]{:S(2)}) async-start(), calls=%async_computation.3 | async-start | bytes 4718592 | tf_op jit(solution)/shard_map/psum | solution.py:52
  170.4 2.0 copy-start
  172.5 91.7 %copy-start.5 = (f32[256,256]{1,0:T(8,128)S(1)}, f32[256,256]{1,0:T(8,128)}, u32[]{:S(2)}) copy-start(f32[256,256]{1,0:T(8,128)} %param.7) | copy-start | bytes 786436
  264.2 7.9 %copy-start.1 = (f32[4096,256]{0,1:T(8,128)S(1)}, f32[4096,256]{0,1:T(8,128)}, u32[]{:S(2)}) copy-start(f32[4096,256]{0,1:T(8,128)} %copy-done) | copy-start | bytes 12582916
  270.1 1.9 copy-start.3
  272.1 4.3 %copy-start.6 = (f32[4096]{0:T(1024)S(1)}, f32[4096]{0:T(1024)}, u32[]{:S(2)}) copy-start(f32[4096]{0:T(1024)} %param.9) | copy-start | bytes 49156
  276.4 15.9 %copy-start.7 = (f32[2048]{0:T(1024)S(1)}, f32[2048]{0:T(1024)}, u32[]{:S(2)}) copy-start(f32[2048]{0:T(1024)} %param.8) | copy-start | bytes 24580
  352.2 6.0 %copy-start.2 = (f32[4096,256]{0,1:T(8,128)S(1)}, f32[4096,256]{0,1:T(8,128)}, u32[]{:S(2)}) copy-start(f32[4096,256]{0,1:T(8,128)} %copy-done) | copy-start | bytes 12582916
  352.2 6.0 %copy-start.4 = (f32[4096,256]{0,1:T(8,128)S(1)}, f32[4096,256]{0,1:T(8,128)}, u32[]{:S(2)}) copy-start(f32[4096,256]{0,1:T(8,128)} %copy-done.3) | copy-start | bytes 12582916
Sparse Core Ops, SparseCore 0:
  10.2 49.8 all-gather.1
  63.7 68.3 all-reduce.5
  167.6 96.5 all-reduce.7
  276.5 74.4 all-reduce.9
where the time goes:
time: 435 us; the launch traced here: 429 us
  waiting for transfers between devices  215 us (49%)
  matrix products  161 us (37%)
  blocking collectives  23.9 us (5%)
  between operations  14.3 us (3%)
  other arithmetic  9.13 us (2%)
  local copies, waits for them, and re-layouts  6.06 us (1%)
    psum x1, waiting for transfers between devices, spread(): return lax.psum(block, axis)  68.8 us
    dot_general x2, matrix products, outer_cols(): lax.dot_general(left, right, (((1,), (1,)), ((), ())), precision=lax.Prec...  62.8 us
    dot_general x12, matrix products, matmul(): return jnp.dot(left, right, precision=lax.Precision.HIGHEST)  59.6 us
    psum x1, waiting for transfers between devices, on_device(): x_rows = lax.psum(matmul(window, v_cols), 'pcol')  57.9 us
    all_gather x1, waiting for transfers between devices, on_device(): gathered = lax.all_gather(panel, 'pcol', axis=0, tiled=True)  50.7 us
    dot_general x2, matrix products, inner_rows(): lax.dot_general(left, right, (((0,), (0,)), ((), ())), precision=lax.Prec...  38.1 us
    psum x1, waiting for transfers between devices, on_device(): w_trans, row_proj = lax.psum((inner_rows(window, v_rows), row_part), 'prow')  37.5 us
    psum x1, blocking collectives, on_device(): lax.psum((matmul(col_check, v_cols), jnp.sum(v_cols, axis=0)), 'pcol')  13.6 us
  transfers between devices with their start and end apart: 4, of which 4 were waited for; matrix products, arithmetic and copies ran while one was open for 12% of the time, Pallas kernels for 0%

commit v1 on v0

v1 whole, which is shorter than its diff:
```python
import functools
import math

import jax
import jax.numpy as jnp
from jax import lax
from jax.experimental import pallas as pl
from jax.experimental.pallas import tpu as pltpu
from jax.sharding import PartitionSpec as P

FULL = lax.Precision.HIGHEST
THREE = lax.Precision.HIGH


def unit_lower(values, row_start):
    rows = row_start + jnp.arange(values.shape[0], dtype=jnp.int32)[:, None]
    cols = jnp.arange(values.shape[1], dtype=jnp.int32)[None, :]
    ones = jnp.where(rows == cols, jnp.ones_like(values), jnp.zeros_like(values))
    return jnp.where(rows > cols, values, ones)


def matmul(left, right, precision=FULL):
    return jnp.dot(left, right, precision=precision)


def inner_rows(left, right, precision=FULL):
    return lax.dot_general(left, right, (((0,), (0,)), ((), ())), precision=precision)


def outer_cols(left, right, precision=FULL):
    return lax.dot_general(left, right, (((1,), (1,)), ((), ())), precision=precision)


MESH = pl.DeviceIdType.MESH


def part(ref, start, size):
    return ref.at[pl.ds(pl.multiple_of(start, 8), size)]


def remote(src, dst, send, recv, prow, pcol):
    return pltpu.make_async_remote_copy(
        src_ref=src, dst_ref=dst, send_sem=send, recv_sem=recv,
        device_id=(prow, pcol), device_id_type=MESH)


def greet(prow, pcol):
    pl.semaphore_signal(pltpu.get_barrier_semaphore(), inc=1, device_id=(prow, pcol), device_id_type=MESH)


def gather_kernel(nr, nc, panel, rows, cols, line_send, sib_send, rows_recv, move_send, move_recv, cols_send, cols_recv):
    p, c = lax.axis_index("prow"), lax.axis_index("pcol")
    pos, core, npos, size = c // 2, c % 2, nc // 2, panel.shape[0]
    sib = c + 1 - 2 * core
    flat, wanted = p * nc + c, c * nr + p
    to_p, to_c, from_p, from_c = flat % nr, flat // nr, wanted // nc, wanted % nc
    here = flat == wanted
    has_left, has_right = pos > 0, pos < npos - 1

    pl.when(has_left)(lambda: greet(p, c - 2))
    pl.when(has_right)(lambda: greet(p, c + 2))
    greet(p, sib)
    for d in range(1, nr):
        greet((p + d) % nr, c)
    pl.when(jnp.logical_not(here))(lambda: greet(from_p, from_c))
    count = has_left.astype(jnp.int32) + has_right.astype(jnp.int32) + 1 + (nr - 1) + jnp.where(here, 0, 1)
    pl.semaphore_wait(pltpu.get_barrier_semaphore(), count)

    def shard(origin):
        return part(rows, origin * size, size)

    def line(origin, slot, step):
        return remote(shard(origin), shard(origin), line_send.at[slot, origin // 2], rows_recv.at[origin], p, c + step)

    def across(origin):
        return remote(shard(origin), shard(origin), sib_send.at[origin // 2], rows_recv.at[origin], p, sib)

    rows[pl.ds(pl.multiple_of(c * size, 8), size)] = panel[...]
    mine = part(cols, p * size, size)
    move = remote(panel, part(cols, to_p * size, size), move_send, move_recv, to_p, to_c)
    pl.when(jnp.logical_not(here))(lambda: move.start())
    pl.when(has_right)(lambda: line(c, 0, 2).start())
    pl.when(has_left)(lambda: line(c, 1, -2).start())
    across(c).start()

    @pl.when(jnp.logical_not(here))
    def _():
        remote(panel, mine, move_send, move_recv, p, sib).wait_recv()

    @pl.when(here)
    def _():
        cols[pl.ds(pl.multiple_of(p * size, 8), size)] = panel[...]

    def spread(d):
        return remote(mine, mine, cols_send.at[d], cols_recv.at[p], (p + d) % nr, c)

    for d in range(1, nr):
        spread(d).start()
    for t in range(1, npos):
        @pl.when(pos >= t)
        def _():
            origin = c - 2 * t
            across(origin).wait_recv()
            pl.when(has_right)(lambda: line(origin, 0, 2).start())
            across(origin).start()

        @pl.when(pos + t < npos)
        def _():
            origin = c + 2 * t
            across(origin).wait_recv()
            pl.when(has_left)(lambda: line(origin, 1, -2).start())
            across(origin).start()
    for i in range(npos):
        across(2 * i + 1 - core).wait_recv()
    for d in range(1, nr):
        origin = (p + d) % nr
        here_part = part(cols, origin * size, size)
        remote(here_part, here_part, cols_send.at[d], cols_recv.at[origin], origin, c).wait_recv()
    for i in range(npos):
        origin = 2 * i + core
        across(origin).wait_send()
        pl.when(jnp.logical_and(has_right, i <= pos))(lambda: line(origin, 0, 2).wait_send())
        pl.when(jnp.logical_and(has_left, i >= pos))(lambda: line(origin, 1, -2).wait_send())
    for d in range(1, nr):
        spread(d).wait_send()
    pl.when(jnp.logical_not(here))(lambda: move.wait_send())


def gather(panel, nr, nc):
    size, width = panel.shape
    dma = pltpu.SemaphoreType.DMA
    vmem = pl.BlockSpec(memory_space=pltpu.VMEM)
    return pl.pallas_call(
        functools.partial(gather_kernel, nr, nc),
        out_shape=(jax.ShapeDtypeStruct((size * nc, width), panel.dtype), jax.ShapeDtypeStruct((size * nr, width), panel.dtype)),
        in_specs=[vmem],
        out_specs=(vmem, vmem),
        scratch_shapes=[dma((2, nc // 2)), dma((nc // 2,)), dma((nc,)), dma, dma, dma((nr,)), dma((nr,))],
        compiler_params=pltpu.CompilerParams(collective_id=0, has_side_effects=True, vmem_limit_bytes=32 * 2**20),
    )(panel)


def on_device(window, panel, factor, col_check, row_check):
    n_rows = lax.axis_size("prow")
    n_cols = lax.axis_size("pcol")
    prow_idx = lax.axis_index("prow")
    pcol_idx = lax.axis_index("pcol")
    rows_blk = window.shape[0]
    cols_blk = window.shape[1]
    order = rows_blk * n_rows
    upper = jnp.triu(factor)
    v_rows, v_cols = gather(panel, n_rows, n_cols)
    v_rows = unit_lower(v_rows, prow_idx * rows_blk)
    v_cols = unit_lower(v_cols, pcol_idx * cols_blk)
    col_proj, col_sums = lax.psum((matmul(col_check, v_cols), jnp.sum(v_cols, axis=0)), "pcol")
    row_part = matmul(row_check, v_rows)
    x_rows = lax.psum(matmul(window, v_cols, THREE), "pcol")
    w_trans, row_proj = lax.psum((inner_rows(window, v_rows, THREE), row_part), "prow")
    y_rows = matmul(x_rows, upper)
    coupled = lax.psum(inner_rows(v_rows, y_rows), "prow")
    m_trans = matmul(w_trans - outer_cols(v_cols, coupled), upper)
    left = jnp.concatenate([y_rows, v_rows], axis=1)
    right = jnp.concatenate([v_cols, m_trans], axis=1)
    new_window = window - outer_cols(left, right, THREE)
    scaled = col_sums / math.sqrt(order)
    new_col = col_check - matmul(v_cols, matmul(col_proj, upper)) - matmul(m_trans, scaled)
    inner = row_proj - matmul(coupled, scaled)
    new_row = row_check - matmul(y_rows, scaled) - matmul(v_rows, matmul(inner, upper))
    return (new_window, new_col, new_row)


def solution(mesh):
    placed = (P("prow", "pcol"), P(("prow", "pcol"), None), P(), P("pcol"), P("prow"))
    return jax.shard_map(
        on_device,
        mesh=mesh,
        in_specs=placed,
        out_specs=(P("prow", "pcol"), P("pcol"), P("prow")),
        check_vma=False,
    )
```

time: 435 us -> 374 us (0.86)
  waiting for transfers between devices: 215 us -> 104 us
  Pallas kernels: 0 us -> 75.6 us
  matrix products: 161 us -> 127 us
  local copies, waits for them, and re-layouts: 6.06 us -> 15.2 us
    pallas_call x0 -> x1, Pallas kernels: none -> 75.6 us  [gather(): pl.pallas_call(functools.partial(gather_kernel, nr, nc), out_shape=(jax.S...]
    psum x3 -> x2, waiting for transfers between devices: 164 us -> 104 us  [the longest x1 71.4 us: on_device(): x_rows = lax.psum(matmul(window, v_cols, THREE), 'pcol')]
    all_gather x1 -> x0, waiting for transfers between devices: 50.7 us -> none  [on_device(): gathered = lax.all_gather(panel, 'pcol', axis=0, tiled=True)]
    dot_general x16, matrix products: 161 us -> 127 us  [the longest x12 61.1 us: matmul(): return jnp.dot(left, right, precision=precision)]
    dot_general x0 -> x2, local copies, waits for them, and re-layouts: none -> 8.82 us  [matmul(): return jnp.dot(left, right, precision=precision)]
  transfers between devices with their start and end apart: 4 -> 2, of which waited for: 4 -> 2; matrix products, arithmetic and copies ran while one was open for 12% -> 11% of each run, Pallas kernels for 0% -> 0%
where the time goes in v1:
time: 374 us; the launch traced here: 368 us
  matrix products  127 us (34%)
  waiting for transfers between devices  104 us (28%)
  Pallas kernels  75.6 us (20%)
  blocking collectives  23.9 us (6%)
  local copies, waits for them, and re-layouts  15.2 us (4%)
  between operations  14.6 us (4%)
  other arithmetic  5.71 us (2%)
    pallas_call x1, Pallas kernels, gather(): pl.pallas_call(functools.partial(gather_kernel, nr, nc), out_shape=(jax.S...  75.6 us
    psum x1, waiting for transfers between devices, on_device(): x_rows = lax.psum(matmul(window, v_cols, THREE), 'pcol')  71.4 us
    dot_general x12, matrix products, matmul(): return jnp.dot(left, right, precision=precision)  61.1 us
    dot_general x2, matrix products, outer_cols(): lax.dot_general(left, right, (((1,), (1,)), ((), ())), precision=precision)  39.3 us
    psum x1, waiting for transfers between devices, on_device(): lax.psum((inner_rows(window, v_rows, THREE), row_part), 'prow')  33.1 us
    dot_general x2, matrix products, inner_rows(): lax.dot_general(left, right, (((0,), (0,)), ((), ())), precision=precision)  27.1 us
    psum x1, blocking collectives, on_device(): lax.psum((matmul(col_check, v_cols), jnp.sum(v_cols, axis=0)), 'pcol')  13.8 us
    psum x1, blocking collectives, on_device(): lax.psum((inner_rows(window, v_rows, THREE), row_part), 'prow')  10.1 us
  transfers between devices with their start and end apart: 2, of which 2 were waited for; matrix products, arithmetic and copies ran while one was open for 11% of the time, Pallas kernels for 0%

profile of v1, /device:TPU:0, one launch (start us, length us, event | category | flops | bytes accessed | tf_op | source)
XLA Modules:
  0.0 367.5 jit_solution(17151160627510298370)
XLA Ops:
  7.2 0.0 all-reduce.5.cloned.1.call-start
  7.2 0.0 copy-start.1
  7.2 1.0 copy-done.1
  8.3 75.6 %shard_map.76 = (f32[4096,256]{1,0:T(8,128)S(1)}, f32[2048,256]{1,0:T(8,128)S(1)}) custom-call(f32[512,256]{1,0:T(8,128)S(1)} %copy-done.1), custom_call_target="tpu_custom_call" | custom-call | tf_op jit(solution)/shard_map/pallas_call | solution.py:133
  83.9 0.0 copy-start
  83.9 2.0 copy-done
  85.9 0.5 fusion.26
  86.4 32.4 %convolution_bitcast_fusion = f32[4096,256]{0,1:T(8,128)} fusion(f32[2048,256]{1,0:T(8,128)S(1)} %get-tuple-element.12, f32[4096,2048]{1,0:T(8,128)} %param.5), kind=kOutput, calls=%fused_computation.4 | convolution fusion | flops 12884901888 | bytes 39845888 | tf_op jit(solution)/shard_map/dot_general | solution.py:23
  118.8 0.0 all-reduce.5.cloned.1.call-update
  118.8 0.6 all-reduce.7.cloned.1.call-start
  119.4 3.9 %select_select_fusion = f32[4096,256]{1,0:T(8,128)} fusion(f32[4096,256]{1,0:T(8,128)} %copy-done, s32[4096]{0:T(1024)S(1)} %iota_add_fusion), kind=kLoop, calls=%fused_computation.8 | loop fusion | flops 4194304 | bytes 8404992 | tf_op jit(solution)/shard_map/jit(_where)/select_n | solution.py:19
  123.3 0.0 copy-start.5
  123.3 19.6 %convolution_bitcast_fusion.1 = f32[2048,256]{0,1:T(8,128)} fusion(f32[4096,256]{1,0:T(8,128)} %select_select_fusion, f32[4096,2048]{1,0:T(8,128)} %param.5), kind=kOutput, calls=%fused_computation.12 | convolution fusion | flops 12884901888 | bytes 39845888 | tf_op jit(solution)/shard_map/dot_general | solution.py:27
  143.0 71.4 %all-reduce.5.cloned.1.call-done = f32[4096,256]{0,1:T(8,128)} async-done(((f32[4096,256]{0,1:T(8,128)}), f32[4096,256]{0,1:T(8,128)}) %all-reduce.5.cloned.1.call-update) | async-done | bytes 4194320 | tf_op jit(solution)/shard_map/psum | solution.py:157
  214.4 0.0 copy-done.5
  214.4 0.0 copy-start.2
  214.4 6.2 %fusion.11 = f32[4096,256]{0,1:T(8,128)S(1)} fusion(f32[4096,256]{0,1:T(8,128)} %all-reduce.5.cloned.1.call-done, f32[256,256]{1,0:T(8,128)S(1)} %copy-done.5, s32[256]{0:T(256)S(1)} %iota_add_fusion.2), kind=kOutput, calls=%fused_computation.21 | convolution fusion | flops 3221356544 | bytes 8651776 | tf_op jit(solution)/shard_map/dot_general | solution.py:23
  220.5 0.0 copy-start.3
  220.6 2.0 copy-done.3
  222.6 0.0 copy-done.2
  222.6 0.0 copy-start.6
  222.6 7.5 %fusion.27 = f32[256,256]{1,0:T(8,128)} fusion(f32[4096,256]{1,0:T(8,128)S(1)} %copy-done.2, f32[4096,256]{0,1:T(8,128)S(1)} %fusion.11), kind=kOutput, calls=%fused_computation.42 | convolution fusion | flops 3221225472 | bytes 8650752 | tf_op jit(solution)/shard_map/dot_general | solution.py:27
  230.0 0.0 copy-start.7
  230.0 0.0 all-reduce.7.cloned.1.call-update
  230.0 0.0 copy-done.6
  230.0 4.2 %fusion.32 = f32[1,256]{1,0:T(1,128)S(1)} fusion(f32[4096,256]{1,0:T(8,128)} %select_select_fusion, f32[4096,1]{0,1:T(1,128)S(1)} %bitcast.50), kind=kOutput, calls=%fused_computation.47 | convolution fusion | flops 12582912 | bytes 4211712 | tf_op jit(solution)/shard_map/dot_general | solution.py:23
  234.3 10.1 %psum.47 = f32[256]{0:T(256)S(1)} all-reduce(f32[256]{0:T(256)S(1)} %bitcast.62), channel_id=1, replica_groups=mesh['prow'=4,'pcol'=8] {'prow'}, use_global_device_ids=true, to_apply=%region_6.7 | all-reduce | flops 256 | bytes 2048 | tf_op jit(solution)/shard_map/psum | solution.py:158
  244.3 0.0 copy-done.7
  244.3 1.1 fusion.28
  245.5 13.8 %all-reduce = (f32[256]{0:T(256)S(1)}, f32[256]{0:T(256)S(1)}) all-reduce(f32[256]{0:T(256)S(1)} %get-tuple-element.11, f32[256]{0:T(256)S(1)} %bitcast.61), channel_id=1, replica_groups=mesh['prow'=4,'pcol'=8] {'pcol'}, use_global_device_ids=true, to_apply=%region_5.6 | all-reduce | flops 512 | bytes 4096 | tf_op jit(solution)/shard_map/psum | solution.py:155
  259.3 0.3 convolution_bitcast_fusion.3
  259.6 1.9 fusion.29
  261.5 5.7 %copy.8 = f32[4096,256]{1,0:T(8,128)} copy(f32[4096,256]{0,1:T(8,128)} %copy-done.3) | data formatting | bytes 8388608 | tf_op jit(solution)/shard_map/dot_general | solution.py:23
  267.1 4.4 %fusion.31 = f32[1,4096]{1,0:T(1,128)S(1)} fusion(f32[4096,256]{0,1:T(8,128)} %copy-done.3, f32[256,1]{0,1:T(1,128)S(1)} %bitcast.56), kind=kOutput, calls=%fused_computation.46 | convolution fusion | flops 12582912 | bytes 4211712 | tf_op jit(solution)/shard_map/dot_general | solution.py:23
  271.6 33.1 %all-reduce.7.cloned.1.call-done = (f32[2048,256]{0,1:T(8,128)}, f32[256,256]{1,0:T(8,128)}) async-done(((f32[2048,256]{0,1:T(8,128)}, f32[256,256]{1,0:T(8,128)}), (f32[2048,256]{0,1:T(8,128)}, f32[256,256]{1,0:T(8,128)})) %all-reduce.7.cloned.1.call-update) | async-done | bytes 2359312 | tf_op jit(solution)/shard_map/psum | solution.py:158
  304.6 1.2 fusion.33
  305.8 3.8 %convolution_subtract_fusion.1 = f32[2048,256]{0,1:T(8,128)S(1)} fusion(f32[2048,256]{0,1:T(8,128)} %get-tuple-element.9, f32[2048,256]{1,0:T(8,128)S(1)} %get-tuple-element.12, f32[256,256]{1,0:T(8,128)} %get-tuple-element.10), kind=kOutput, calls=%fused_computation.11 | convolution fusion | flops 1611137024 | bytes 6553600 | tf_op jit(solution)/shard_map/dot_general | solution.py:31
  309.7 2.1 fusion.9
  311.9 0.0 copy-start.4
  311.9 1.3 copy-done.4
  313.2 1.2 fusion.30
  314.4 3.1 copy.9
  317.5 0.3 convolution_bitcast_fusion.2
  317.8 5.8 %fusion.34 = f32[1,4096]{1,0:T(1,128)S(1)} fusion(f32[4096,256]{1,0:T(8,128)} %select_select_fusion, f32[256,1]{0,1:T(1,128)S(1)} %convolution_bitcast_fusion.2), kind=kOutput, calls=%fused_computation.49 | convolution fusion | flops 12582912 | bytes 4211712 | tf_op jit(solution)/shard_map/dot_general | solution.py:23
  323.6 0.6 subtract_subtract_fusion.1
  324.2 0.6 subtract_subtract_fusion
  324.8 35.4 %convolution_subtract_fusion = f32[4096,2048]{1,0:T(8,128)} fusion(f32[4096,2048]{1,0:T(8,128)} %param.5, f32[4096,256]{1,0:T(8,128)} %select_select_fusion, f32[4096,256]{1,0:T(8,128)} %copy.8, f32[2048,256]{1,0:T(8,128)} %copy.9, f32[2048,256]{1,0:T(8,128)S(1)} %get-tuple-element.12), kind=kOutput, calls=%fused_computation | convolution fusion | flops 25781338112 | bytes 79691776 | tf_op jit(solution)/shard_map/dot_general | solution.py:31
  (5 shorter events, 0.0 us)
Async XLA Ops:
  7.2 207.2 %all-reduce.5.cloned.1.call-start = ((), (), s32[]{:S(2)}) async-start(), calls=%async_computation | async-start | bytes 8388608 | tf_op jit(solution)/shard_map/psum | solution.py:157
  7.2 1.0 copy-start.1
  83.9 2.0 copy-start
  118.8 185.8 %all-reduce.7.cloned.1.call-start = ((), (), s32[]{:S(2)}) async-start(), calls=%async_computation.1 | async-start | bytes 4718592 | tf_op jit(solution)/shard_map/psum | solution.py:158
  123.3 91.0 %copy-start.5 = (f32[256,256]{1,0:T(8,128)S(1)}, f32[256,256]{1,0:T(8,128)}, u32[]{:S(2)}) copy-start(f32[256,256]{1,0:T(8,128)} %param.7) | copy-start | bytes 786436
  214.4 8.2 %copy-start.2 = (f32[4096,256]{1,0:T(8,128)S(1)}, f32[4096,256]{1,0:T(8,128)}, u32[]{:S(2)}) copy-start(f32[4096,256]{1,0:T(8,128)} %select_select_fusion) | copy-start | bytes 12582916
  220.5 2.0 copy-start.3
  222.6 7.5 %copy-start.6 = (f32[4096]{0:T(1024)S(1)}, f32[4096]{0:T(1024)}, u32[]{:S(2)}) copy-start(f32[4096]{0:T(1024)} %param.9) | copy-start | bytes 49156
  230.0 14.3 %copy-start.7 = (f32[2048]{0:T(1024)S(1)}, f32[2048]{0:T(1024)}, u32[]{:S(2)}) copy-start(f32[2048]{0:T(1024)} %param.8) | copy-start | bytes 24580
  311.9 1.3 copy-start.4
Sparse Core Ops, SparseCore 0:
  118.9 95.4 all-reduce.4
  230.2 74.4 all-reduce.6
